TPU v7x, 512 devices: a whole 4x4x16 slice. The times are simulated.
512 devices in a mesh: frames: 32 (over y, x, core), atoms: 16 (over z).
Axes of the slice: x: 4, y: 4, z: 16, core: 2. Of those that a mesh axis runs over, the one named last changes fastest.
Arguments:
- frames: float32 [2048, 3, 6144], P('frames', None, 'atoms'), may hold values from -45 to 45, as said below
- reference_structure: float32 [3, 6144], P(None, 'atoms'), may hold values from -15 to 15
Outputs:
- covariance: float32 [3, 6144, 3, 6144], P(None, 'frames', None, 'atoms')
- mean_structure: float32 [3, 6144], P(None, 'atoms')
Inputs may be any that keep to these rules, and one draw needn't show every extreme that they name: `frames`: every frame, once centered, has a cross-covariance with the centered reference_structure of positive determinant whose singular values lie within a factor of 20 of one another.
All inputs are finite; a program needn't handle non-finite values.
Results may differ from a plain program's by a relative error of at most 0.0003.
Values may be sent and summed in bfloat16 or wider, within the bound.
A program may use at most 64 MiB of HBM per device.

v0:
```python
import jax
import jax.numpy as jnp
from jax import lax
from jax.sharding import Mesh
from jax.sharding import PartitionSpec as P

ATOMS = 6144
ITERS = 2
POLAR = 8
FRAMES = ("frames_0", "frames_1", "frames_2")


def copy_for_each(array, axis):
    copies = jnp.broadcast_to(array, (lax.axis_size(axis), *array.shape))
    return lax.all_to_all(copies, axis, split_axis=0, concat_axis=0, tiled=True)


def over_copies(array, axis):
    everything = copy_for_each(array, axis)
    return jnp.sum(everything, axis=0)


def in_one(arrays, axis):
    vector, at, finished = (jnp.concatenate([a.reshape(-1) for a in arrays]), 0, [])
    total = over_copies(vector, axis)
    for a in arrays:
        finished.append(total[at : at + a.size].reshape(a.shape))
        at += a.size
    return tuple(finished)


def in_blocks(array, dim, devices):
    lengths = array.shape
    blocks = array.reshape(*lengths[:dim], devices, lengths[dim] // devices, *lengths[dim + 1 :])
    return jnp.moveaxis(blocks, dim, 0)


def laid_out(blocks, dim):
    blocks = jnp.moveaxis(blocks, 0, dim)
    lengths = blocks.shape
    return blocks.reshape(*lengths[:dim], lengths[dim] * lengths[dim + 1], *lengths[dim + 2 :])


def exchange_in_order(blocks, axes, turns):
    lengths = [lax.axis_size(a) for a in axes]
    blocks = blocks.reshape(*lengths, *blocks.shape[1:])
    for k in turns:
        blocks = lax.all_to_all(blocks, axes[k], split_axis=k, concat_axis=k, tiled=True)
    return blocks.reshape(-1, *blocks.shape[len(axes) :])


def core_and_chips(array, groups, turns, split_dim, concat_dim):
    devices = lax.axis_size(groups[0]) * lax.axis_size(groups[1])
    blocks = in_blocks(array, split_dim, devices)
    return laid_out(exchange_in_order(blocks, groups, turns), concat_dim)


def polar_factor(cross):
    factor = jnp.sqrt(3.0 / jnp.sum(cross * cross, axis=(0, 1)))
    matrix = cross * factor[None, None, :]
    for turn in range(POLAR):
        entries = [[matrix[i, j] for j in range(3)] for i in range(3)]
        cofactor = [
            [
                entries[(i + 1) % 3][(j + 1) % 3] * entries[(i + 2) % 3][(j + 2) % 3]
                - entries[(i + 1) % 3][(j + 2) % 3] * entries[(i + 2) % 3][(j + 1) % 3]
                for j in range(3)
            ]
            for i in range(3)
        ]
        determinant = (
            entries[0][0] * cofactor[0][0]
            + entries[0][1] * cofactor[0][1]
            + entries[0][2] * cofactor[0][2]
        )
        inverse = jnp.stack([jnp.stack(cofactor[i]) for i in range(3)]) / determinant[None, None, :]
        matrix = 0.5 * (matrix + inverse)
    return matrix


def contract_frames(left_rows, right_rows):
    return lax.dot_general(
        left_rows, right_rows, (((0,), (0,)), ((), ())), preferred_element_type=jnp.float32
    )


def body(frames, reference_structure):
    highest = lax.Precision.HIGHEST
    mean_now = reference_structure
    count_all = frames.shape[0] * lax.axis_size(FRAMES)
    for iteration in range(ITERS):
        sum_coords, sum_cross, sum_mean = in_one(
            (
                jnp.sum(frames, axis=2),
                jnp.einsum("fca,da->cdf", frames, mean_now, precision=highest),
                jnp.sum(mean_now, axis=1),
            ),
            "atoms",
        )
        centroid = sum_coords / ATOMS
        cross = sum_cross - centroid.T[:, None, :] * sum_mean[None, :, None]
        shifted = frames - centroid[:, :, None]
        rotation = polar_factor(cross)
        aligned = jnp.einsum("cdf,fca->fda", rotation, shifted, precision=highest)
        mean_now = over_copies(jnp.sum(aligned, axis=0), FRAMES) / count_all
    deviation = (aligned - mean_now[None]).astype(jnp.bfloat16)
    column_atoms = frames.shape[2]
    row_count = column_atoms * lax.axis_size("atoms") // lax.axis_size(FRAMES)
    own_rows = lax.all_gather(deviation, "atoms", axis=2, tiled=True)
    row_panel = core_and_chips(own_rows, (("frames_0", "frames_1"), "frames_2"), (1, 0), 2, 0)
    row_flat = row_panel.reshape(row_panel.shape[0], 3 * row_count)
    piece = lax.all_gather(deviation, FRAMES, axis=0, tiled=True)
    product = contract_frames(row_flat, piece.reshape(piece.shape[0], 3 * column_atoms))
    covariance = (product / count_all).reshape(3, row_count, 3, column_atoms)
    return (covariance, mean_now)


def solution(mesh):
    finer = Mesh(
        mesh.devices.reshape(4, 4, 2, mesh.shape["atoms"]),
        ("frames_0", "frames_1", "frames_2", "atoms"),
    )
    return jax.shard_map(
        body,
        mesh=finer,
        in_specs=(P(FRAMES, None, "atoms"), P(None, "atoms")),
        out_specs=(P(None, FRAMES, None, "atoms"), P(None, "atoms")),
        check_vma=False,
    )
```

profile of v0, /device:TPU:2, one launch (start us, length us, event | category | flops | bytes accessed | tf_op | source)
XLA Modules:
  0.0 281.3 jit_solution(8115866642797572257)
XLA Ops:
  7.2 0.8 reduce_sum.99
  8.1 1.1 reduce_sum.98
  9.1 1.4 convolution_bitcast_fusion.2
  11.1 27.7 %all_to_all.32 = f32[16,1,771]{2,1,0:T(1,128)S(1)} all-to-all(f32[16,1,771]{2,1,0:T(1,128)S(1)} %broadcast_in_dim.8), channel_id=1, replica_groups=mesh['frames_0'=4,'frames_1'=4,'frames_2'=2,'atoms'=16] {'atoms'}, dimensions={0} | all-to-all | bytes 98688 | tf_op jit(solution)/shard_map/all_to_all | solution.py:15
  40.7 1.3 convolution_bitcast_fusion.1
  42.1 14.4 %all_to_all.33 = f32[32,3,384]{2,1,0:T(4,128)S(1)} all-to-all(f32[32,3,384]{2,1,0:T(4,128)S(1)} %broadcast_in_dim.9), channel_id=1, replica_groups=mesh['frames_0'=4,'frames_1'=4,'frames_2'=2,'atoms'=16] {'frames_0','fra..., dimensions={0} | all-to-all | bytes 294912 | tf_op jit(solution)/shard_map/all_to_all | solution.py:15
  56.7 1.4 convolution_bitcast_fusion
  58.4 15.9 %all_to_all.34 = f32[16,1,771]{2,1,0:T(1,128)S(1)} all-to-all(f32[16,1,771]{2,1,0:T(1,128)S(1)} %broadcast_in_dim.10), channel_id=1, replica_groups=mesh['frames_0'=4,'frames_1'=4,'frames_2'=2,'atoms'=16] {'atoms'}, dimensions={0} | all-to-all | bytes 98688 | tf_op jit(solution)/shard_map/all_to_all | solution.py:15
  76.6 1.1 fusion.33
  77.7 11.5 %all_to_all.35 = f32[32,3,384]{2,1,0:T(4,128)S(1)} all-to-all(f32[32,3,384]{2,1,0:T(4,128)S(1)} %broadcast_in_dim.11), channel_id=1, replica_groups=mesh['frames_0'=4,'frames_1'=4,'frames_2'=2,'atoms'=16] {'frames_0','fra..., dimensions={0} | all-to-all | bytes 294912 | tf_op jit(solution)/shard_map/all_to_all | solution.py:15
  90.1 1.6 copy.60
  91.7 75.2 %all-gather.3.cloned.1.call-done = bf16[64,3,6144]{2,1,0:T(4,128)(2,1)} async-done(((bf16[64,3,384]{2,1,0:T(4,128)(2,1)}), bf16[64,3,6144]{2,1,0:T(4,128)(2,1)}) %all-gather.3.cloned.1.call-update) | async-done | bytes 2359312 | tf_op jit(solution)/shard_map/all_gather | solution.py:109
  166.9 3.6 %copy.56 = bf16[64,3,6144]{2,0,1:T(8,128)(2,1)S(1)} copy(bf16[64,3,6144]{2,1,0:T(4,128)(2,1)} %all-gather.3.cloned.1.call-done) | data formatting | bytes 4718592 | tf_op jit(solution)/shard_map/all_gather | solution.py:109
  170.5 4.6 %reshape.5858 = bf16[64,3,32,192]{3,2,0,1:T(8,128)(2,1)} reshape(bf16[64,3,6144]{2,0,1:T(8,128)(2,1)S(1)} %copy.56) | data formatting | bytes 4718592 | tf_op jit(solution)/shard_map/reshape | solution.py:34
  175.1 4.3 %reshape.5859 = bf16[16,2,64,3,192]{4,1,0,2,3:T(2,128)(2,1)S(1)} reshape(bf16[32,64,3,192]{3,0,1,2:T(8,128)(2,1)} %bitcast.395) | data formatting | bytes 4718592 | tf_op jit(solution)/shard_map/reshape | solution.py:46
  179.4 1.8 copy.57
  181.2 6.3 %all_to_all.36 = bf16[16,2,64,3,192]{4,2,3,0,1:T(8,128)(2,1)S(1)} all-to-all(bf16[16,2,64,3,192]{4,2,3,0,1:T(8,128)(2,1)S(1)} %copy.57), channel_id=1, replica_groups=mesh['frames_0'=4,'frames_1'=4,'frames_2'=2,'atoms'=16] {'frames_2'}, dimensions={1} | all-to-all | bytes 4718592 | tf_op jit(solution)/shard_map/all_to_all | solution.py:48
  187.8 53.9 %all_to_all.37 = bf16[16,2,64,3,192]{4,2,3,1,0:T(8,128)(2,1)S(1)} all-to-all(bf16[16,2,64,3,192]{4,2,3,1,0:T(8,128)(2,1)S(1)} %copy.58), channel_id=1, replica_groups=mesh['frames_0'=4,'frames_1'=4,'frames_2'=2,'atoms'=16] {'frames_0','fra..., dimensions={0} | all-to-all | bytes 4718592 | tf_op jit(solution)/shard_map/all_to_all | solution.py:48
  241.7 5.0 %copy.59 = bf16[16,2,64,3,192]{4,3,2,1,0:T(4,128)(2,1)} copy(bf16[16,2,64,3,192]{4,2,3,1,0:T(8,128)(2,1)S(1)} %all_to_all.37) | data formatting | bytes 4718592 | tf_op jit(solution)/shard_map/all_to_all | solution.py:48
  246.8 8.0 %reshape_reshape_reshape.3 = bf16[2048,576]{1,0:T(8,128)(2,1)S(1)} reshape(bf16[16,2,64,3,192]{4,3,2,1,0:T(4,128)(2,1)} %copy.59) | data formatting | bytes 4718592 | tf_op jit(solution)/shard_map/reshape;reshape;reshape | solution.py:111
  254.8 6.7 %copy.61 = bf16[2048,3,384]{0,2,1:T(8,128)(2,1)} copy(bf16[2048,3,384]{2,0,1:T(8,128)(2,1)} %all-gather.5.cloned.1.call-done) | data formatting | bytes 9437184 | tf_op jit(solution)/shard_map/all_gather | solution.py:112
  261.6 7.4 %convolution_multiply_fusion = f32[576,1152]{1,0:T(8,128)} fusion(bf16[2048,576]{1,0:T(8,128)(2,1)S(1)} %reshape_reshape_reshape.3, bf16[2048,1152]{0,1:T(8,128)(2,1)} %bitcast.396), kind=kOutput, calls=%fused_computation | convolution fusion | flops 2718572544 | bytes 9732096 | tf_op jit(solution)/shard_map/dot_general | solution.py:82
  269.0 3.7 %reshape.5861 = f32[3,192,3,384]{3,2,1,0:T(4,128)S(1)} reshape(f32[576,1152]{1,0:T(8,128)} %convolution_multiply_fusion) | data formatting | bytes 5308416 | tf_op jit(solution)/shard_map/reshape | solution.py:114
  272.7 1.7 copy.62
  (143 shorter events, 6.1 us)
Async XLA Ops:
  7.2 69.3 %copy-start = (f32[64,3,384]{2,0,1:T(8,128)S(1)}, f32[64,3,384]{2,0,1:T(8,128)}, u32[]{:S(2)}) copy-start(f32[64,3,384]{2,0,1:T(8,128)} %param.2) | copy-start | bytes 884740
  7.2 159.8 %all-gather.3.cloned.1.call-start = ((), (), s32[]{:S(2)}) async-start(), calls=%async_computation.6 | async-start | bytes 3342336 | tf_op jit(solution)/shard_map/all_gather | solution.py:109
  89.3 81.3 %copy-start.1 = (f32[3,384]{1,0:T(4,128)}, f32[3,384]{1,0:T(4,128)S(1)}, u32[]{:S(2)}) copy-start(f32[3,384]{1,0:T(4,128)S(1)} %broadcast_multiply_fusion) | copy-start | bytes 13828
  90.1 164.8 %all-gather.5.cloned.1.call-start = ((), (), s32[]{:S(2)}) async-start(), calls=%async_computation.7 | async-start | bytes 4866048 | tf_op jit(solution)/shard_map/all_gather | solution.py:112
Sparse Core Ops, SparseCore 0:
  90.2 76.7 all-gather.2
  170.1 73.4 all-gather.4
where the time goes:
time: 282 us; the launch traced here: 281 us
  blocking collectives  130 us (46%)
  waiting for transfers between devices  75.2 us (27%)
  local copies, waits for them, and re-layouts  43.1 us (15%)
  between operations  14.7 us (5%)
  matrix products  12.7 us (5%)
  other arithmetic  5.79 us (2%)
    all_gather x1, waiting for transfers between devices, body(): own_rows = lax.all_gather(deviation, 'atoms', axis=2, tiled=True)  75.2 us
    all_to_all x4, blocking collectives, copy_for_each(): return lax.all_to_all(copies, axis, split_axis=0, concat_axis=0, tiled=True)  69.5 us
    all_to_all x2, blocking collectives, exchange_in_order(): lax.all_to_all(blocks, axes[k], split_axis=k, concat_axis=k, tiled=True)  60.2 us
    another operation x1, local copies, waits for them, and re-layouts, body(): row_flat = row_panel.reshape(row_panel.shape[0], 3 * row_count)  8.03 us
    dot_general x1, matrix products, contract_frames(): lax.dot_general(left_rows, right_rows, (((0,), (0,)), ((), ())), preferre...  7.42 us
    all_gather x1, local copies, waits for them, and re-layouts, body(): piece = lax.all_gather(deviation, FRAMES, axis=0, tiled=True)  6.75 us
    reshape x2, local copies, waits for them, and re-layouts, exchange_in_order(): blocks = blocks.reshape(*lengths, *blocks.shape[1:])  6.04 us
  transfers between devices with their start and end apart: 2, of which 1 were waited for; matrix products, arithmetic and copies ran while one was open for 10% of the time, Pallas kernels for 0%

commit v1 on v0

--- a/solution.py
+++ b/solution.py
@@ -106,7 +106,9 @@
     deviation = (aligned - mean_now[None]).astype(jnp.bfloat16)
     column_atoms = frames.shape[2]
     row_count = column_atoms * lax.axis_size("atoms") // lax.axis_size(FRAMES)
-    own_rows = lax.all_gather(deviation, "atoms", axis=2, tiled=True)
+    u_next = jnp.stack([deviation for _ in range(lax.axis_size("atoms"))], axis=0)
+    far_arr = lax.all_to_all(u_next, "atoms", split_axis=0, concat_axis=0)
+    own_rows = jnp.concatenate(far_arr, 2)
     row_panel = core_and_chips(own_rows, (("frames_0", "frames_1"), "frames_2"), (1, 0), 2, 0)
     row_flat = row_panel.reshape(row_panel.shape[0], 3 * row_count)
     piece = lax.all_gather(deviation, FRAMES, axis=0, tiled=True)

time: 282 us -> 311 us (1.10)
  the two profiles are of different devices: /device:TPU:2 before, /device:TPU:1 now
where the time goes in v1:
time: 311 us; the launch traced here: 310 us
  waiting for transfers between devices  144 us (46%)
  blocking collectives  78.6 us (25%)
  local copies, waits for them, and re-layouts  45.1 us (15%)
  between operations  14.7 us (5%)
  matrix products  12.7 us (4%)
  starting transfers between devices  9.78 us (3%)
  other arithmetic  5.13 us (2%)
    all_to_all x1, waiting for transfers between devices, body(): far_arr = lax.all_to_all(u_next, 'atoms', split_axis=0, concat_axis=0)  103 us
    all_to_all x4, blocking collectives, copy_for_each(): return lax.all_to_all(copies, axis, split_axis=0, concat_axis=0, tiled=True)  71.7 us
    all_to_all x1, waiting for transfers between devices, exchange_in_order(): lax.all_to_all(blocks, axes[k], split_axis=k, concat_axis=k, tiled=True)  40.8 us
    another operation x1, local copies, waits for them, and re-layouts, body(): row_flat = row_panel.reshape(row_panel.shape[0], 3 * row_count)  8.03 us
    dot_general x1, matrix products, contract_frames(): lax.dot_general(left_rows, right_rows, (((0,), (0,)), ((), ())), preferre...  7.42 us
    all_to_all x2, local copies, waits for them, and re-layouts, exchange_in_order(): lax.all_to_all(blocks, axes[k], split_axis=k, concat_axis=k, tiled=True)  7.03 us
    all_to_all x1, blocking collectives, exchange_in_order(): lax.all_to_all(blocks, axes[k], split_axis=k, concat_axis=k, tiled=True)  6.86 us
    all_gather x1, local copies, waits for them, and re-layouts, body(): piece = lax.all_gather(deviation, FRAMES, axis=0, tiled=True)  6.73 us
  transfers between devices with their start and end apart: 3, of which 2 were waited for; matrix products, arithmetic and copies ran while one was open for 7% of the time, Pallas kernels for 0%

profile of v1, /device:TPU:1, one launch (start us, length us, event | category | flops | bytes accessed | tf_op | source)
XLA Modules:
  0.0 310.3 jit_solution(6222511275006475489)
XLA Ops:
  9.1 1.4 convolution_bitcast_fusion.2
  11.0 27.2 %all_to_all.37 = f32[16,1,771]{2,1,0:T(1,128)S(1)} all-to-all(f32[16,1,771]{2,1,0:T(1,128)S(1)} %broadcast_in_dim.8), channel_id=1, replica_groups=mesh['frames_0'=4,'frames_1'=4,'frames_2'=2,'atoms'=16] {'atoms'}, dimensions={0} | all-to-all | bytes 98688 | tf_op jit(solution)/shard_map/all_to_all | solution.py:15
  40.2 1.3 convolution_bitcast_fusion.1
  41.5 17.2 %all_to_all.38 = f32[32,3,384]{2,1,0:T(4,128)S(1)} all-to-all(f32[32,3,384]{2,1,0:T(4,128)S(1)} %broadcast_in_dim.9), channel_id=1, replica_groups=mesh['frames_0'=4,'frames_1'=4,'frames_2'=2,'atoms'=16] {'frames_0','fra..., dimensions={0} | all-to-all | bytes 294912 | tf_op jit(solution)/shard_map/all_to_all | solution.py:15
  58.9 1.4 convolution_bitcast_fusion
  60.6 14.2 %all_to_all.39 = f32[16,1,771]{2,1,0:T(1,128)S(1)} all-to-all(f32[16,1,771]{2,1,0:T(1,128)S(1)} %broadcast_in_dim.10), channel_id=1, replica_groups=mesh['frames_0'=4,'frames_1'=4,'frames_2'=2,'atoms'=16] {'atoms'}, dimensions={0} | all-to-all | bytes 98688 | tf_op jit(solution)/shard_map/all_to_all | solution.py:15
  78.2 13.2 %all_to_all.40 = f32[32,3,384]{2,1,0:T(4,128)S(1)} all-to-all(f32[32,3,384]{2,1,0:T(4,128)S(1)} %broadcast_in_dim.11), channel_id=1, replica_groups=mesh['frames_0'=4,'frames_1'=4,'frames_2'=2,'atoms'=16] {'frames_0','fra..., dimensions={0} | all-to-all | bytes 294912 | tf_op jit(solution)/shard_map/all_to_all | solution.py:15
  91.6 1.8 stack.611
  93.4 3.7 %all-to-all-start.4 = ((bf16[16,64,3,384]{3,1,2,0:T(8,128)(2,1)}), bf16[16,64,3,384]{3,1,2,0:T(8,128)(2,1)S(1)}, u32[]{:S(2)}, u32[]{:S(2)}) async-start(bf16[16,64,3,384]{3,1,2,0:T(8,128)(2,1)} %stack.611), calls=%async_computation.4 | async-start | bytes 4718592 | tf_op jit(solution)/shard_map/all_to_all | solution.py:110
  97.9 102.7 %all-to-all-done.4 = bf16[16,64,3,384]{3,1,2,0:T(8,128)(2,1)S(1)} async-done(((bf16[16,64,3,384]{3,1,2,0:T(8,128)(2,1)}), bf16[16,64,3,384]{3,1,2,0:T(8,128)(2,1)S(1)}, u32[]{:S(2)}, u32[]{:S(2)}) %all-to-all-start.4) | async-done | bytes 2359328 | tf_op jit(solution)/shard_map/all_to_all | solution.py:110
  200.6 2.8 copy.72
  203.4 5.6 %reshape_reshape.3 = bf16[64,3,32,192]{3,2,1,0:T(8,128)(2,1)} reshape(bf16[64,3,16,384]{3,2,1,0:T(8,128)(2,1)} %copy.72) | data formatting | bytes 4718592 | tf_op jit(solution)/shard_map/reshape;reshape | solution.py:34
  209.0 4.3 %reshape.5861 = bf16[16,2,64,3,192]{4,1,0,3,2:T(2,128)(2,1)S(1)} reshape(bf16[32,64,3,192]{3,0,2,1:T(8,128)(2,1)} %bitcast.396) | data formatting | bytes 4718592 | tf_op jit(solution)/shard_map/reshape | solution.py:46
  213.3 1.8 copy.73
  215.1 6.9 %all_to_all.41 = bf16[16,2,64,3,192]{4,2,3,0,1:T(8,128)(2,1)S(1)} all-to-all(bf16[16,2,64,3,192]{4,2,3,0,1:T(8,128)(2,1)S(1)} %copy.73), channel_id=1, replica_groups=mesh['frames_0'=4,'frames_1'=4,'frames_2'=2,'atoms'=16] {'frames_2'}, dimensions={1} | all-to-all | bytes 4718592 | tf_op jit(solution)/shard_map/all_to_all | solution.py:48
  221.9 2.1 copy.74
  224.0 6.0 %all-to-all-start.6 = ((bf16[16,2,64,3,192]{4,2,3,1,0:T(8,128)(2,1)}), bf16[16,2,64,3,192]{4,2,3,1,0:T(8,128)(2,1)S(1)}, u32[]{:S(2)}, u32[]{:S(2)}) async-start(bf16[16,2,64,3,192]{4,2,3,1,0:T(8,128)(2,1)} %copy.74), calls=%async_computation.6 | async-start | bytes 6291456 | tf_op jit(solution)/shard_map/all_to_all | solution.py:48
  230.0 6.7 %copy.77 = bf16[2048,3,384]{0,2,1:T(8,128)(2,1)} copy(bf16[2048,3,384]{2,0,1:T(8,128)(2,1)} %all-gather.2.cloned.1.call-done) | data formatting | bytes 9437184 | tf_op jit(solution)/shard_map/all_gather | solution.py:114
  236.8 40.8 %all-to-all-done.6 = bf16[16,2,64,3,192]{4,2,3,1,0:T(8,128)(2,1)S(1)} async-done(((bf16[16,2,64,3,192]{4,2,3,1,0:T(8,128)(2,1)}), bf16[16,2,64,3,192]{4,2,3,1,0:T(8,128)(2,1)S(1)}, u32[]{:S(2)}, u32[]{:S(2)}) %all-to-all-start.6) | async-done | bytes 2359328 | tf_op jit(solution)/shard_map/all_to_all | solution.py:48
  277.6 5.0 %copy.75 = bf16[16,2,64,3,192]{4,3,2,1,0:T(4,128)(2,1)} copy(bf16[16,2,64,3,192]{4,2,3,1,0:T(8,128)(2,1)S(1)} %all-to-all-done.6) | data formatting | bytes 4718592 | tf_op jit(solution)/shard_map/all_to_all | solution.py:48
  282.5 8.0 %reshape_reshape_reshape.3 = bf16[2048,576]{1,0:T(8,128)(2,1)S(1)} reshape(bf16[16,2,64,3,192]{4,3,2,1,0:T(4,128)(2,1)} %copy.75) | data formatting | bytes 4718592 | tf_op jit(solution)/shard_map/reshape;reshape;reshape | solution.py:113
  290.6 7.4 %convolution_multiply_fusion = f32[576,1152]{1,0:T(8,128)} fusion(bf16[2048,576]{1,0:T(8,128)(2,1)S(1)} %reshape_reshape_reshape.3, bf16[2048,1152]{0,1:T(8,128)(2,1)} %bitcast.398), kind=kOutput, calls=%fused_computation | convolution fusion | flops 2718572544 | bytes 9732096 | tf_op jit(solution)/shard_map/dot_general | solution.py:82
  298.0 3.7 %reshape.5863 = f32[3,192,3,384]{3,2,1,0:T(4,128)S(1)} reshape(f32[576,1152]{1,0:T(8,128)} %convolution_multiply_fusion) | data formatting | bytes 5308416 | tf_op jit(solution)/shard_map/reshape | solution.py:116
  301.8 1.7 copy.78
  (146 shorter events, 8.6 us)
Async XLA Ops:
  7.2 69.8 %copy-start = (f32[64,3,384]{2,0,1:T(8,128)S(1)}, f32[64,3,384]{2,0,1:T(8,128)}, u32[]{:S(2)}) copy-start(f32[64,3,384]{2,0,1:T(8,128)} %param.2) | copy-start | bytes 884740
  91.5 1.9 copy-start.2
  91.6 1.8 copy-start.1
  93.4 107.2 %all-to-all-start.4 = ((bf16[16,64,3,384]{3,1,2,0:T(8,128)(2,1)}), bf16[16,64,3,384]{3,1,2,0:T(8,128)(2,1)S(1)}, u32[]{:S(2)}, u32[]{:S(2)}) async-start(bf16[16,64,3,384]{3,1,2,0:T(8,128)(2,1)} %stack.611), calls=%async_computation.4 | async-start | bytes 4718592 | tf_op jit(solution)/shard_map/all_to_all | solution.py:110
  97.1 132.9 %all-gather.2.cloned.1.call-start = ((), (), s32[]{:S(2)}) async-start(), calls=%async_computation.7 | async-start | bytes 4866048 | tf_op jit(solution)/shard_map/all_gather | solution.py:114
  224.0 53.6 %all-to-all-start.6 = ((bf16[16,2,64,3,192]{4,2,3,1,0:T(8,128)(2,1)}), bf16[16,2,64,3,192]{4,2,3,1,0:T(8,128)(2,1)S(1)}, u32[]{:S(2)}, u32[]{:S(2)}) async-start(bf16[16,2,64,3,192]{4,2,3,1,0:T(8,128)(2,1)} %copy.74), calls=%async_computation.6 | async-start | bytes 6291456 | tf_op jit(solution)/shard_map/all_to_all | solution.py:48
Sparse Core Ops, SparseCore 0:
  101.1 59.8 all-gather.1
